TPU v7x, 512 devices: a whole 4x4x16 slice. The times are simulated.
512 devices in a mesh: panel: 64 (over x, z), obs: 8 (over y, core).
Axes of the slice: x: 4, y: 4, z: 16, core: 2. Of those that a mesh axis runs over, the one named last changes fastest.
Arguments:
- donor: bfloat16 [512, 125, 4, 1024], P('panel', None, None, 'obs'), may hold values from -6 to 6
- donor_elem: int32 [8192], P('obs'), may hold values from 0 to 1023, as said below
- local_coords: float32 [3, 8192], P(None, 'obs'), may hold values from -1 to 1
- owner: int32 [8192], replicated, may hold values from 0 to 63, as said below
- weights: bfloat16 [1024, 4, 4, 8192], P('obs', None, None, 'panel'), may hold values from -0.015625 to 0.015625
- offsets: int32 [8, 64], P('obs', 'panel'), may hold values from 0 to 256
Outputs:
- pressure: float32 [512, 1024], P('panel', 'obs')
Inputs may be any that keep to these rules, and one draw needn't show every extreme that they name: `donor_elem`: point i lies in a donor element of the i // 1024-th block of 128 elements. Every owner owns exactly 128 points. Within each of the 8 aligned blocks of 1024 points an owner appears either 44 times or 128 / 8 - 128 / 32 times, and exactly one block holds 44 of its points.
All inputs are finite; a program needn't handle non-finite values.
Results may differ from a plain program's by a relative error of at most 0.0029.
Values may be sent and summed in bfloat16 or wider, within the bound.
A program may use at most 64 MiB of HBM per device.

v0:
```python
import jax
import jax.numpy as jnp
from jax import lax
from jax.sharding import PartitionSpec as P

BAND = 4
OBLK = 128
PTILE = 128
NODE_SPOTS = (-1.0, -0.5, 0.0, 0.5, 1.0)


def lagrange_table(coords):
    factors = []
    for direction in range(3):
        coord_row = coords[direction]
        columns = []
        for node_one in range(5):
            weighting = jnp.ones_like(coord_row)
            for node_two in range(5):
                if node_two != node_one:
                    weighting = weighting * (
                        (coord_row - NODE_SPOTS[node_two])
                        / (NODE_SPOTS[node_one] - NODE_SPOTS[node_two])
                    )
            columns.append(weighting)
        factors.append(jnp.stack(columns))
    node_table = (
        factors[0][:, None, None, :] * factors[1][None, :, None, :] * factors[2][None, None, :, :]
    )
    return node_table.reshape(125, coords.shape[1])


def body(donor, donor_elem, local_coords, owner, weights, offsets):
    share_index = lax.axis_index("obs")
    elem_local = donor_elem - share_index * donor.shape[3]
    node_table = lagrange_table(local_coords)

    def one_time(moment):
        values = jnp.take(moment, elem_local, axis=2)
        return jnp.sum(node_table[:, None, :] * values, axis=0).astype(jnp.bfloat16)

    local_sources = lax.map(one_time, donor)
    order = jnp.argsort(owner, stable=True)
    everything = lax.all_gather(local_sources, "obs", axis=2, tiled=True)
    outgoing = jnp.take(everything, order, axis=2)
    sources = lax.all_to_all(outgoing, "panel", split_axis=2, concat_axis=0, tiled=True)
    total_time = sources.shape[0]
    front = total_time // 2 + BAND - 1
    padded = jnp.pad(sources, ((front, 0), (0, 0), (0, 0)))
    delay_steps = offsets[0, 0]
    base = 0 + front - delay_steps
    stacked = jnp.stack(
        [lax.dynamic_slice_in_dim(padded, base - delay, total_time, 0) for delay in range(BAND)],
        axis=1,
    )
    stacked = stacked.reshape(total_time, BAND * padded.shape[1] * PTILE)
    weight_tile = weights
    weight_tile = weight_tile.reshape(OBLK, stacked.shape[1])
    running = lax.dot_general(
        stacked, weight_tile, (((1,), (1,)), ((), ())), preferred_element_type=jnp.float32
    )
    pressure = lax.psum_scatter(running, "panel", scatter_dimension=0, tiled=True)
    return pressure


def solution(mesh):
    return jax.shard_map(
        body,
        mesh=mesh,
        in_specs=(
            P("panel", None, None, "obs"),
            P("obs"),
            P(None, "obs"),
            P(),
            P("obs", None, None, "panel"),
            P("obs", "panel"),
        ),
        out_specs=P("panel", "obs"),
        check_vma=False,
    )
```

profile of v0, /device:TPU:8, one launch (start us, length us, event | category | flops | bytes accessed | tf_op | source)
XLA Modules:
  0.0 636.2 jit_solution(15393408633668595031)
XLA Ops:
  6.5 7.6 %sort.17 = (s32[8192]{0:T(1024)}, s32[8192]{0:T(1024)S(1)}) sort(s32[8192]{0:T(1024)} %param.11, s32[8192]{0:T(1024)S(1)} %iota.4), dimensions={0}, to_apply=%region_0.1 | sort | flops 106496 | bytes 131072 | tf_op jit(solution)/shard_map/jit(argsort)/sort | solution.py:43
  14.2 1.0 multiply_multiply_fusion.10
  15.1 0.7 broadcast_subtract_fusion
  16.0 160.1 %while.11 = (s32[]{:T(128)}, bf16[8,4,1024]{2,0,1:T(8,128)(2,1)S(1)}, s32[1024]{0:T(1024)S(1)}, bf16[8,125,4,128]{3,2,1,0:T(4,128)(2,1)}, f32[5,1024]{1,0:T(8,12...) while((s32[]{:T(128)}, bf16[8,4,1024]{2,0,1:T(8,128)(2,1)S(1)}, s32[1024]{0:T(1024)S(1)}, ...), condition=%wide.region_3.4_spmd.clone, body=%wide.region_1.0_spmd.clone.sunk | while | flops 2182146 | bytes 6846565 | solution.py:42
  16.0 1.0 constant_dynamic-slice_fusion.3
  17.4 0.2 copy.38
  17.6 3.6 gather_fusion
  21.2 14.5 %fusion.23 = bf16[4,1024]{0,1:T(8,128)(2,1)S(1)} fusion(bf16[1024,125,4]{1,2,0:T(4,128)(2,1)S(1)} %gather_fusion, f32[125,1024]{0,1:T(8,128)S(1)} %copy.38, pred[1024]{0:T(1024)(128)(4,1)S(1)} %compare_and_fusion.3), kind=kLoop, calls=%fused_computation.4.clone.1 | loop fusion | flops 2043904 | bytes 1545216 | tf_op jit(solution)/shard_map/while/body/eval_jaxpr/reduce_sum | solution.py:40
  35.7 0.2 copy.39
  36.0 1.0 constant_dynamic-slice_fusion.3
  37.4 0.2 copy.38
  37.6 3.6 gather_fusion
  41.2 14.5 %fusion.23 = bf16[4,1024]{0,1:T(8,128)(2,1)S(1)} fusion(bf16[1024,125,4]{1,2,0:T(4,128)(2,1)S(1)} %gather_fusion, f32[125,1024]{0,1:T(8,128)S(1)} %copy.38, pred[1024]{0:T(1024)(128)(4,1)S(1)} %compare_and_fusion.3), kind=kLoop, calls=%fused_computation.4.clone.1 | loop fusion | flops 2043904 | bytes 1545216 | tf_op jit(solution)/shard_map/while/body/eval_jaxpr/reduce_sum | solution.py:40
  55.7 0.2 copy.39
  56.1 1.0 constant_dynamic-slice_fusion.3
  57.0 0.2 copy.37
  57.4 0.2 copy.38
  57.6 3.6 gather_fusion
  61.2 14.5 %fusion.23 = bf16[4,1024]{0,1:T(8,128)(2,1)S(1)} fusion(bf16[1024,125,4]{1,2,0:T(4,128)(2,1)S(1)} %gather_fusion, f32[125,1024]{0,1:T(8,128)S(1)} %copy.38, pred[1024]{0:T(1024)(128)(4,1)S(1)} %compare_and_fusion.3), kind=kLoop, calls=%fused_computation.4.clone.1 | loop fusion | flops 2043904 | bytes 1545216 | tf_op jit(solution)/shard_map/while/body/eval_jaxpr/reduce_sum | solution.py:40
  75.7 0.2 copy.39
  76.1 1.0 constant_dynamic-slice_fusion.3
  77.0 0.2 copy.37
  77.4 0.2 copy.38
  77.6 3.6 gather_fusion
  81.2 14.5 %fusion.23 = bf16[4,1024]{0,1:T(8,128)(2,1)S(1)} fusion(bf16[1024,125,4]{1,2,0:T(4,128)(2,1)S(1)} %gather_fusion, f32[125,1024]{0,1:T(8,128)S(1)} %copy.38, pred[1024]{0:T(1024)(128)(4,1)S(1)} %compare_and_fusion.3), kind=kLoop, calls=%fused_computation.4.clone.1 | loop fusion | flops 2043904 | bytes 1545216 | tf_op jit(solution)/shard_map/while/body/eval_jaxpr/reduce_sum | solution.py:40
  95.7 0.2 copy.39
  96.1 1.0 constant_dynamic-slice_fusion.3
  97.1 0.2 copy.37
  97.4 0.2 copy.38
  97.6 3.6 gather_fusion
  101.2 14.5 %fusion.23 = bf16[4,1024]{0,1:T(8,128)(2,1)S(1)} fusion(bf16[1024,125,4]{1,2,0:T(4,128)(2,1)S(1)} %gather_fusion, f32[125,1024]{0,1:T(8,128)S(1)} %copy.38, pred[1024]{0:T(1024)(128)(4,1)S(1)} %compare_and_fusion.3), kind=kLoop, calls=%fused_computation.4.clone.1 | loop fusion | flops 2043904 | bytes 1545216 | tf_op jit(solution)/shard_map/while/body/eval_jaxpr/reduce_sum | solution.py:40
  115.7 0.2 copy.39
  116.1 1.0 constant_dynamic-slice_fusion.3
  117.1 0.2 copy.37
  117.4 0.2 copy.38
  117.7 3.6 gather_fusion
  121.2 14.5 %fusion.23 = bf16[4,1024]{0,1:T(8,128)(2,1)S(1)} fusion(bf16[1024,125,4]{1,2,0:T(4,128)(2,1)S(1)} %gather_fusion, f32[125,1024]{0,1:T(8,128)S(1)} %copy.38, pred[1024]{0:T(1024)(128)(4,1)S(1)} %compare_and_fusion.3), kind=kLoop, calls=%fused_computation.4.clone.1 | loop fusion | flops 2043904 | bytes 1545216 | tf_op jit(solution)/shard_map/while/body/eval_jaxpr/reduce_sum | solution.py:40
  135.7 0.2 copy.39
  136.1 1.0 constant_dynamic-slice_fusion.3
  137.1 0.2 copy.37
  137.5 0.2 copy.38
  137.7 3.6 gather_fusion
  141.3 14.5 %fusion.23 = bf16[4,1024]{0,1:T(8,128)(2,1)S(1)} fusion(bf16[1024,125,4]{1,2,0:T(4,128)(2,1)S(1)} %gather_fusion, f32[125,1024]{0,1:T(8,128)S(1)} %copy.38, pred[1024]{0:T(1024)(128)(4,1)S(1)} %compare_and_fusion.3), kind=kLoop, calls=%fused_computation.4.clone.1 | loop fusion | flops 2043904 | bytes 1545216 | tf_op jit(solution)/shard_map/while/body/eval_jaxpr/reduce_sum | solution.py:40
  155.8 0.2 copy.39
  156.2 1.0 constant_dynamic-slice_fusion.3
  157.5 0.2 copy.38
  157.7 3.6 gather_fusion
  161.3 14.5 %fusion.23 = bf16[4,1024]{0,1:T(8,128)(2,1)S(1)} fusion(bf16[1024,125,4]{1,2,0:T(4,128)(2,1)S(1)} %gather_fusion, f32[125,1024]{0,1:T(8,128)S(1)} %copy.38, pred[1024]{0:T(1024)(128)(4,1)S(1)} %compare_and_fusion.3), kind=kLoop, calls=%fused_computation.4.clone.1 | loop fusion | flops 2043904 | bytes 1545216 | tf_op jit(solution)/shard_map/while/body/eval_jaxpr/reduce_sum | solution.py:40
  175.8 0.2 copy.39
  176.1 15.8 %all_gather.3 = bf16[8,4,8192]{2,0,1:T(8,128)(2,1)S(1)} all-gather(bf16[8,4,1024]{2,0,1:T(8,128)(2,1)S(1)} %get-tuple-element.34), channel_id=1, replica_groups=mesh['panel'=64,'obs'=8] {'obs'}, dimensions={2}, use_global_device_ids=true | all-gather | bytes 589824 | tf_op jit(solution)/shard_map/all_gather | solution.py:44
  191.9 8.1 %copy.24 = bf16[8,4,8192]{0,1,2:T(4,128)(2,1)} copy(bf16[8,4,8192]{2,0,1:T(8,128)(2,1)S(1)} %all_gather.3) | data formatting | bytes 1048576 | tf_op jit(solution)/shard_map/all_gather | solution.py:44
  200.0 59.6 %gather_fusion.1 = bf16[8192,8,4]{1,2,0:T(4,128)(2,1)} fusion(bf16[8,4,8192]{0,1,2:T(4,128)(2,1)} %copy.24, s32[8192]{0:T(1024)S(1)} %fusion.19), kind=kCustom, calls=%fused_computation.1 | custom fusion | bytes 1081344 | tf_op jit(solution)/shard_map/jit(_take)/gather | solution.py:45
  259.7 30.9 %fusion.21 = bf16[8192,4,8]{2,1,0:T(4,128)(2,1)} fusion(bf16[8192,8,4]{1,2,0:T(4,128)(2,1)} %gather_fusion.1, pred[8192]{0:T(1024)(128)(4,1)S(1)} %compare_and_fusion.1), kind=kLoop, calls=%fused_computation.65 | loop fusion | flops 262144 | bytes 1056768
  290.6 11.2 %reshape.84 = bf16[64,2,2048]{2,1,0:T(2,128)(2,1)} reshape(bf16[8192,4,8]{2,1,0:T(4,128)(2,1)} %fusion.21) | data formatting | bytes 1048576
  301.8 16.1 %all-to-all-start = ((bf16[64,2,2048]{2,1,0:T(2,128)(2,1)}), bf16[64,2,2048]{2,1,0:T(2,128)(2,1)S(1)}, u32[]{:S(2)}, u32[]{:S(2)}) async-start(bf16[64,2,2048]{2,1,0:T(2,128)(2,1)} %reshape.84), calls=%async_computation | async-start | bytes 1048576 | tf_op jit(solution)/shard_map/all_to_all | solution.py:46
  317.9 0.2 all-reduce.4.cloned.1.call-start
  318.8 31.5 %all-to-all-done = bf16[64,2,2048]{2,1,0:T(2,128)(2,1)S(1)} async-done(((bf16[64,2,2048]{2,1,0:T(2,128)(2,1)}), bf16[64,2,2048]{2,1,0:T(2,128)(2,1)S(1)}, u32[]{:S(2)}, u32[]{:S(2)}) %all-to-all-start) | async-done | bytes 524320 | tf_op jit(solution)/shard_map/all_to_all | solution.py:46
  350.3 10.9 %reshape.85 = bf16[8192,4,8]{2,1,0:T(4,128)(2,1)} reshape(bf16[64,2,2048]{2,1,0:T(2,128)(2,1)S(1)} %all-to-all-done) | data formatting | bytes 1048576
  361.1 9.9 %copy.25 = bf16[64,8,4,128]{3,1,0,2:T(8,128)(2,1)S(1)} copy(bf16[64,8,4,128]{1,2,3,0:T(4,128)(2,1)} %bitcast.53) | data formatting | bytes 1048576 | tf_op jit(solution)/shard_map/all_to_all | solution.py:46
  371.0 0.9 fusion.14
  371.9 1.4 fusion.11
  373.4 1.3 dynamic-slice
  375.3 252.8 %all-reduce.4.cloned.1.call-done = f32[512,128]{1,0:T(8,128)} async-done(((f32[512,128]{1,0:T(8,128)}), f32[512,128]{1,0:T(8,128)}) %all-reduce.4.cloned.1.call-update) | async-done | bytes 262160
  628.1 1.3 constant_dynamic-slice_fusion.1
  (62 shorter events, 3.2 us)
Async XLA Ops:
  6.5 365.4 %copy-start = (bf16[128,4,4,128]{3,2,1,0:T(4,128)(2,1)S(1)}, bf16[128,4,4,128]{3,2,1,0:T(4,128)(2,1)}, u32[]{:S(2)}) copy-start(bf16[128,4,4,128]{3,2,1,0:T(4,128)(2,1)} %param.12) | copy-start | bytes 1572868
  301.8 48.5 %all-to-all-start = ((bf16[64,2,2048]{2,1,0:T(2,128)(2,1)}), bf16[64,2,2048]{2,1,0:T(2,128)(2,1)S(1)}, u32[]{:S(2)}, u32[]{:S(2)}) async-start(bf16[64,2,2048]{2,1,0:T(2,128)(2,1)} %reshape.84), calls=%async_computation | async-start | bytes 1048576 | tf_op jit(solution)/shard_map/all_to_all | solution.py:46
  317.9 310.2 %all-reduce.4.cloned.1.call-start = ((), (), s32[]{:S(2)}) async-start(), calls=%async_computation.1 | async-start | bytes 524288
Sparse Core Ops, SparseCore 0:
  373.5 254.5 all-reduce.3
where the time goes:
time: 637 us; the launch traced here: 636 us
  waiting for transfers between devices  284 us (45%)
  other arithmetic  157 us (25%)
  local copies, waits for them, and re-layouts  146 us (23%)
  starting transfers between devices  16.3 us (3%)
  blocking collectives  15.8 us (2%)
  between operations  14.8 us (2%)
    unnamed x2, waiting for transfers between devices  253 us
    reduce_sum x8, other arithmetic, one_time(): return jnp.sum(node_table[:, None, :] * values, axis=0).astype(jnp.bfloat16)  116 us
    gather x1, local copies, waits for them, and re-layouts, body(): outgoing = jnp.take(everything, order, axis=2)  59.6 us
    all_to_all x1, waiting for transfers between devices, body(): lax.all_to_all(outgoing, 'panel', split_axis=2, concat_axis=0, tiled=True)  31.5 us
    unnamed x1, other arithmetic  30.9 us
    gather x8, local copies, waits for them, and re-layouts, one_time(): values = jnp.take(moment, elem_local, axis=2)  28.6 us
    unnamed x6, local copies, waits for them, and re-layouts  24.6 us
    all_to_all x1, starting transfers between devices, body(): lax.all_to_all(outgoing, 'panel', split_axis=2, concat_axis=0, tiled=True)  16.1 us
  transfers between devices with their start and end apart: 2, of which 2 were waited for; matrix products, arithmetic and copies ran while one was open for 0% of the time, Pallas kernels for 0%

commit v1 on v0

--- a/solution.py
+++ b/solution.py
@@ -7,6 +7,22 @@
 OBLK = 128
 PTILE = 128
 NODE_SPOTS = (-1.0, -0.5, 0.0, 0.5, 1.0)
+
+
+def gather_around(x, axis, dim):
+    ways, here, step = (lax.axis_size(axis), lax.axis_index(axis), x.shape[dim])
+    lengths = [n * ways if d == dim else n for d, n in enumerate(x.shape)]
+    full = lax.dynamic_update_slice_in_dim(jnp.zeros(lengths, x.dtype), x, here * step, axis=dim)
+    going_up = going_down = x
+    for far in range(1, ways // 2 + 1):
+        going_up = lax.ppermute(going_up, axis, [(d, (d + 1) % ways) for d in range(ways)])
+        full = lax.dynamic_update_slice_in_dim(full, going_up, (here - far) % ways * step, axis=dim)
+        if 2 * far < ways:
+            going_down = lax.ppermute(going_down, axis, [(d, (d - 1) % ways) for d in range(ways)])
+            full = lax.dynamic_update_slice_in_dim(
+                full, going_down, (here + far) % ways * step, axis=dim
+            )
+    return full
 
 
 def lagrange_table(coords):
@@ -41,7 +57,7 @@
 
     local_sources = lax.map(one_time, donor)
     order = jnp.argsort(owner, stable=True)
-    everything = lax.all_gather(local_sources, "obs", axis=2, tiled=True)
+    everything = gather_around(local_sources, "obs", 2)
     outgoing = jnp.take(everything, order, axis=2)
     sources = lax.all_to_all(outgoing, "panel", split_axis=2, concat_axis=0, tiled=True)
     total_time = sources.shape[0]

time: 637 us -> 657 us (1.031)
  local copies, waits for them, and re-layouts: 146 us -> 172 us
  blocking collectives: 15.8 us -> 0 us
    all_gather x1 -> x0, blocking collectives: 15.8 us -> none  [body(): everything = lax.all_gather(local_sources, 'obs', axis=2, tiled=True)]
    dynamic_update_slice x0 -> x8, local copies, waits for them, and re-layouts: none -> 10.9 us  [the longest x4 5.45 us: gather_around(): lax.dynamic_update_slice_in_dim(full, going_up, (here - far) % ways * ste...]
    while x0 -> x2, local copies, waits for them, and re-layouts: none -> 10.2 us  [body(): local_sources = lax.map(one_time, donor)]
    ppermute x0 -> x7, starting transfers between devices: none -> 8.87 us  [the longest x3 8.85 us: gather_around(): lax.ppermute(going_down, axis, [(d, (d - 1) % ways) for d in range(ways)])]
    all_gather x1 -> x0, local copies, waits for them, and re-layouts: 8.11 us -> none  [body(): everything = lax.all_gather(local_sources, 'obs', axis=2, tiled=True)]
    unnamed x6 -> x8, local copies, waits for them, and re-layouts: 24.6 us -> 24.6 us
  transfers between devices with their start and end apart: 2 -> 9, of which waited for: 2 -> 3; matrix products, arithmetic and copies ran while one was open for 0% -> 5% of each run, Pallas kernels for 0% -> 0%
where the time goes in v1:
time: 657 us; the launch traced here: 656 us
  waiting for transfers between devices  288 us (44%)
  local copies, waits for them, and re-layouts  172 us (26%)
  other arithmetic  156 us (24%)
  starting transfers between devices  22.7 us (3%)
  between operations  14.9 us (2%)
    unnamed x2, waiting for transfers between devices  254 us
    reduce_sum x8, other arithmetic, one_time(): return jnp.sum(node_table[:, None, :] * values, axis=0).astype(jnp.bfloat16)  116 us
    gather x1, local copies, waits for them, and re-layouts, body(): outgoing = jnp.take(everything, order, axis=2)  59.7 us
    all_to_all x1, waiting for transfers between devices, body(): lax.all_to_all(outgoing, 'panel', split_axis=2, concat_axis=0, tiled=True)  31.1 us
    unnamed x1, other arithmetic  30.9 us
    gather x8, local copies, waits for them, and re-layouts, one_time(): values = jnp.take(moment, elem_local, axis=2)  28.6 us
    unnamed x8, local copies, waits for them, and re-layouts  24.6 us
    all_to_all x1, starting transfers between devices, body(): lax.all_to_all(outgoing, 'panel', split_axis=2, concat_axis=0, tiled=True)  13.8 us
  transfers between devices with their start and end apart: 9, of which 3 were waited for; matrix products, arithmetic and copies ran while one was open for 5% of the time, Pallas kernels for 0%

profile of v1, /device:TPU:8, one launch (start us, length us, event | category | flops | bytes accessed | tf_op | source)
XLA Modules:
  0.0 655.8 jit_solution(4042926453490158697)
XLA Ops:
  6.5 1.0 multiply_multiply_fusion.10
  7.6 0.7 broadcast_subtract_fusion
  8.4 163.2 %while.11 = (s32[]{:T(128)}, bf16[8,4,1024]{1,2,0:T(8,128)(2,1)}, s32[1024]{0:T(1024)S(1)}, bf16[8,125,4,128]{3,2,1,0:T(4,128)(2,1)}, f32[5,1024]{1,0:T(8,128)S(1)}, /*index=5*/f32[5,5,1024]{2,1,0:T(8,128)S(1)}, s32[]{:T(128)}) while((s32[]{:T(128)}, bf16[8,4,1024]{1,2,0:T(8,128)(2,1)}, s32[1024]{0:T(1024)S(1)}, ...), condition=%wide.region_3.4_spmd.clone, body=%wide.region_1.0_spmd.clone.sunk | while | flops 2182146 | bytes 7084625 | solution.py:58
  8.4 1.0 constant_dynamic-slice_fusion.3
  9.5 3.6 gather_fusion
  13.5 14.5 %fusion.23 = bf16[4,1024]{0,1:T(8,128)(2,1)S(1)} fusion(bf16[1024,125,4]{1,2,0:T(4,128)(2,1)S(1)} %gather_fusion, f32[125,1024]{0,1:T(8,128)S(1)} %copy.49, pred[1024]{0:T(1024)(128)(4,1)S(1)} %compare_and_fusion.3), kind=kLoop, calls=%fused_computation.4.clone.1 | loop fusion | flops 2043904 | bytes 1545216 | tf_op jit(solution)/shard_map/while/body/eval_jaxpr/reduce_sum | solution.py:56
  28.0 0.7 bitcast_dynamic-update-slice_fusion.2
  28.8 0.9 constant_dynamic-slice_fusion.3
  29.9 3.6 gather_fusion
  33.9 14.5 %fusion.23 = bf16[4,1024]{0,1:T(8,128)(2,1)S(1)} fusion(bf16[1024,125,4]{1,2,0:T(4,128)(2,1)S(1)} %gather_fusion, f32[125,1024]{0,1:T(8,128)S(1)} %copy.49, pred[1024]{0:T(1024)(128)(4,1)S(1)} %compare_and_fusion.3), kind=kLoop, calls=%fused_computation.4.clone.1 | loop fusion | flops 2043904 | bytes 1545216 | tf_op jit(solution)/shard_map/while/body/eval_jaxpr/reduce_sum | solution.py:56
  48.4 0.7 bitcast_dynamic-update-slice_fusion.2
  49.1 0.9 constant_dynamic-slice_fusion.3
  50.3 3.6 gather_fusion
  54.3 14.5 %fusion.23 = bf16[4,1024]{0,1:T(8,128)(2,1)S(1)} fusion(bf16[1024,125,4]{1,2,0:T(4,128)(2,1)S(1)} %gather_fusion, f32[125,1024]{0,1:T(8,128)S(1)} %copy.49, pred[1024]{0:T(1024)(128)(4,1)S(1)} %compare_and_fusion.3), kind=kLoop, calls=%fused_computation.4.clone.1 | loop fusion | flops 2043904 | bytes 1545216 | tf_op jit(solution)/shard_map/while/body/eval_jaxpr/reduce_sum | solution.py:56
  68.8 0.7 bitcast_dynamic-update-slice_fusion.2
  69.5 0.9 constant_dynamic-slice_fusion.3
  70.7 3.6 gather_fusion
  74.7 14.5 %fusion.23 = bf16[4,1024]{0,1:T(8,128)(2,1)S(1)} fusion(bf16[1024,125,4]{1,2,0:T(4,128)(2,1)S(1)} %gather_fusion, f32[125,1024]{0,1:T(8,128)S(1)} %copy.49, pred[1024]{0:T(1024)(128)(4,1)S(1)} %compare_and_fusion.3), kind=kLoop, calls=%fused_computation.4.clone.1 | loop fusion | flops 2043904 | bytes 1545216 | tf_op jit(solution)/shard_map/while/body/eval_jaxpr/reduce_sum | solution.py:56
  89.2 0.7 bitcast_dynamic-update-slice_fusion.2
  89.9 0.9 constant_dynamic-slice_fusion.3
  91.1 3.6 gather_fusion
  95.1 14.5 %fusion.23 = bf16[4,1024]{0,1:T(8,128)(2,1)S(1)} fusion(bf16[1024,125,4]{1,2,0:T(4,128)(2,1)S(1)} %gather_fusion, f32[125,1024]{0,1:T(8,128)S(1)} %copy.49, pred[1024]{0:T(1024)(128)(4,1)S(1)} %compare_and_fusion.3), kind=kLoop, calls=%fused_computation.4.clone.1 | loop fusion | flops 2043904 | bytes 1545216 | tf_op jit(solution)/shard_map/while/body/eval_jaxpr/reduce_sum | solution.py:56
  109.6 0.7 bitcast_dynamic-update-slice_fusion.2
  110.3 0.9 constant_dynamic-slice_fusion.3
  111.5 3.6 gather_fusion
  115.5 14.5 %fusion.23 = bf16[4,1024]{0,1:T(8,128)(2,1)S(1)} fusion(bf16[1024,125,4]{1,2,0:T(4,128)(2,1)S(1)} %gather_fusion, f32[125,1024]{0,1:T(8,128)S(1)} %copy.49, pred[1024]{0:T(1024)(128)(4,1)S(1)} %compare_and_fusion.3), kind=kLoop, calls=%fused_computation.4.clone.1 | loop fusion | flops 2043904 | bytes 1545216 | tf_op jit(solution)/shard_map/while/body/eval_jaxpr/reduce_sum | solution.py:56
  130.0 0.7 bitcast_dynamic-update-slice_fusion.2
  130.7 0.9 constant_dynamic-slice_fusion.3
  131.9 3.6 gather_fusion
  135.9 14.5 %fusion.23 = bf16[4,1024]{0,1:T(8,128)(2,1)S(1)} fusion(bf16[1024,125,4]{1,2,0:T(4,128)(2,1)S(1)} %gather_fusion, f32[125,1024]{0,1:T(8,128)S(1)} %copy.49, pred[1024]{0:T(1024)(128)(4,1)S(1)} %compare_and_fusion.3), kind=kLoop, calls=%fused_computation.4.clone.1 | loop fusion | flops 2043904 | bytes 1545216 | tf_op jit(solution)/shard_map/while/body/eval_jaxpr/reduce_sum | solution.py:56
  150.4 0.7 bitcast_dynamic-update-slice_fusion.2
  151.1 0.9 constant_dynamic-slice_fusion.3
  152.3 3.6 gather_fusion
  156.3 14.5 %fusion.23 = bf16[4,1024]{0,1:T(8,128)(2,1)S(1)} fusion(bf16[1024,125,4]{1,2,0:T(4,128)(2,1)S(1)} %gather_fusion, f32[125,1024]{0,1:T(8,128)S(1)} %copy.49, pred[1024]{0:T(1024)(128)(4,1)S(1)} %compare_and_fusion.3), kind=kLoop, calls=%fused_computation.4.clone.1 | loop fusion | flops 2043904 | bytes 1545216 | tf_op jit(solution)/shard_map/while/body/eval_jaxpr/reduce_sum | solution.py:56
  170.8 0.7 bitcast_dynamic-update-slice_fusion.2
  171.5 2.0 copy.28
  173.6 1.7 collective-permute-start.1
  175.3 8.2 %copy.27 = bf16[8,4,1024]{0,1,2:T(4,128)(2,1)S(1)} copy(bf16[8,4,1024]{1,2,0:T(8,128)(2,1)} %get-tuple-element.34) | data formatting | bytes 131072 | tf_op jit(solution)/shard_map/while | solution.py:58
  183.5 6.8 %sort.17 = (s32[8192]{0:T(1024)}, s32[8192]{0:T(1024)S(1)}) sort(s32[8192]{0:T(1024)S(1)} %copy-done.1, s32[8192]{0:T(1024)S(1)} %iota.4), dimensions={0}, to_apply=%region_0.1 | sort | flops 106496 | bytes 131072 | tf_op jit(solution)/shard_map/jit(argsort)/sort | solution.py:59
  190.3 5.4 broadcast_in_dim.34
  195.7 1.4 constant_dynamic-update-slice_fusion.7
  197.8 1.4 constant_dynamic-update-slice_fusion.6
  199.1 0.7 copy.31
  199.8 1.4 constant_dynamic-update-slice_fusion.5
  201.2 4.1 collective-permute-start.3
  206.0 1.3 constant_dynamic-update-slice_fusion.4
  208.0 1.3 constant_dynamic-update-slice_fusion.3
  209.3 3.0 collective-permute-start.5
  213.0 1.4 constant_dynamic-update-slice_fusion.2
  215.0 1.4 constant_dynamic-update-slice_fusion.1
  216.4 2.8 collective-permute-done.6
  219.9 1.4 constant_dynamic-update-slice_fusion
  221.2 59.7 %gather_fusion.1 = bf16[8192,8,4]{1,2,0:T(4,128)(2,1)} fusion(bf16[8,4,8192]{0,1,2:T(4,128)(2,1)} %constant_dynamic-update-slice_fusion, s32[8192]{0:T(1024)S(1)} %fusion.19), kind=kCustom, calls=%fused_computation.1 | custom fusion | bytes 1081344 | tf_op jit(solution)/shard_map/jit(_take)/gather | solution.py:61
  280.9 30.9 %fusion.21 = bf16[8192,4,8]{2,1,0:T(4,128)(2,1)} fusion(bf16[8192,8,4]{1,2,0:T(4,128)(2,1)} %gather_fusion.1, pred[8192]{0:T(1024)(128)(4,1)S(1)} %compare_and_fusion.1), kind=kLoop, calls=%fused_computation.73 | loop fusion | flops 262144 | bytes 1056768
  311.9 11.2 %reshape.84 = bf16[64,2,2048]{2,1,0:T(2,128)(2,1)} reshape(bf16[8192,4,8]{2,1,0:T(4,128)(2,1)} %fusion.21) | data formatting | bytes 1048576
  323.0 13.8 %all-to-all-start = ((bf16[64,2,2048]{2,1,0:T(2,128)(2,1)}), bf16[64,2,2048]{2,1,0:T(2,128)(2,1)S(1)}, u32[]{:S(2)}, u32[]{:S(2)}) async-start(bf16[64,2,2048]{2,1,0:T(2,128)(2,1)} %reshape.84), calls=%async_computation | async-start | bytes 1048576 | tf_op jit(solution)/shard_map/all_to_all | solution.py:62
  337.5 31.1 %all-to-all-done = bf16[64,2,2048]{2,1,0:T(2,128)(2,1)S(1)} async-done(((bf16[64,2,2048]{2,1,0:T(2,128)(2,1)}), bf16[64,2,2048]{2,1,0:T(2,128)(2,1)S(1)}, u32[]{:S(2)}, u32[]{:S(2)}) %all-to-all-start) | async-done | bytes 524320 | tf_op jit(solution)/shard_map/all_to_all | solution.py:62
  368.7 10.9 %reshape.85 = bf16[8192,4,8]{2,1,0:T(4,128)(2,1)} reshape(bf16[64,2,2048]{2,1,0:T(2,128)(2,1)S(1)} %all-to-all-done) | data formatting | bytes 1048576
  379.6 9.9 %copy.42 = bf16[8,4,64,128]{3,0,2,1:T(8,128)(2,1)S(1)} copy(bf16[8,4,64,128]{0,1,3,2:T(4,128)(2,1)} %bitcast.53) | data formatting | bytes 1048576 | tf_op jit(solution)/shard_map/all_to_all | solution.py:62
  389.5 0.9 fusion.14
  390.4 1.4 fusion.11
  391.8 1.3 dynamic-slice
  393.7 254.0 %all-reduce.4.cloned.1.call-done = f32[512,128]{1,0:T(8,128)} async-done(((f32[512,128]{1,0:T(8,128)}), f32[512,128]{1,0:T(8,128)}) %all-reduce.4.cloned.1.call-update) | async-done | bytes 262160
  647.7 1.3 constant_dynamic-slice_fusion.1
  (86 shorter events, 8.9 us)
Async XLA Ops:
  6.5 383.8 %copy-start = (bf16[128,4,4,128]{3,2,1,0:T(4,128)(2,1)S(1)}, bf16[128,4,4,128]{3,2,1,0:T(4,128)(2,1)}, u32[]{:S(2)}) copy-start(bf16[128,4,4,128]{3,2,1,0:T(4,128)(2,1)} %param.12) | copy-start | bytes 1572868
  8.3 175.2 %copy-start.1 = (s32[8192]{0:T(1024)S(1)}, s32[8192]{0:T(1024)}, u32[]{:S(2)}) copy-start(s32[8192]{0:T(1024)} %param.11) | copy-start | bytes 98308
  173.6 23.5 %collective-permute-start = (bf16[8,4,1024]{2,0,1:T(8,128)(2,1)S(1)}, bf16[8,4,1024]{2,0,1:T(8,128)(2,1)S(1)}, u32[]{:S(2)}, u32[]{:S(2)}) collective-permute-start(bf16[8,4,1024]{2,0,1:T(8,128)(2,1)S(1)} %copy.28), channel_id=1, source_target_pairs={{0,1},{1,2},{2,3},{3,4},{4,5},{5,6},{6,7},{7,0},{8,9},{9,10},{10,1... | collective-permute-start | bytes 196616 | tf_op jit(solution)/shard_map/ppermute | solution.py:18
  173.6 25.6 %collective-permute-start.1 = (bf16[8,4,1024]{2,0,1:T(8,128)(2,1)S(1)}, bf16[8,4,1024]{2,0,1:T(8,128)(2,1)S(1)}, u32[]{:S(2)}, u32[]{:S(2)}) collective-permute-start(bf16[8,4,1024]{2,0,1:T(8,128)(2,1)S(1)} %copy.28), channel_id=1, source_target_pairs={{0,7},{1,0},{2,1},{3,2},{4,3},{5,4},{6,5},{7,6},{8,15},{9,8},{10,9... | collective-permute-start | bytes 196616 | tf_op jit(solution)/shard_map/ppermute | solution.py:21
  199.1 6.2 collective-permute-start.2
  201.2 6.1 collective-permute-start.3
  207.3 5.0 collective-permute-start.4
  209.3 5.0 collective-permute-start.5
  214.3 4.9 collective-permute-start.6
  323.0 45.6 %all-to-all-start = ((bf16[64,2,2048]{2,1,0:T(2,128)(2,1)}), bf16[64,2,2048]{2,1,0:T(2,128)(2,1)S(1)}, u32[]{:S(2)}, u32[]{:S(2)}) async-start(bf16[64,2,2048]{2,1,0:T(2,128)(2,1)} %reshape.84), calls=%async_computation | async-start | bytes 1048576 | tf_op jit(solution)/shard_map/all_to_all | solution.py:62
  336.8 310.9 %all-reduce.4.cloned.1.call-start = ((), (), s32[]{:S(2)}) async-start(), calls=%async_computation.1 | async-start | bytes 524288
Sparse Core Ops, SparseCore 0:
  391.9 255.7 all-reduce.3
